TPU v7x, 512 devices: a whole 4x8x8 slice. The times are simulated.
512 devices in a mesh: vis: 64 (over y, z), chan: 8 (over x, core).
Axes of the slice: x: 4, y: 8, z: 8, core: 2. Of those that a mesh axis runs over, the one named last changes fastest.
Arguments:
- model: float32 [2, 256, 1024], P(None, 'vis', 'chan'), may hold values from -6 to 6
- kernels: float32 [2, 32, 8], replicated, may hold values from -1.5 to 1.5
- vis_data: float32 [2, 8, 524288], P(None, 'chan', 'vis'), may hold values from -6 to 6
- vis_weight: float32 [8, 524288], P('chan', 'vis'), may hold values from 0.2 to 2
- tile_list: int32 [8, 64, 16], P('chan', 'vis'), may hold values from 0 to 255, as said below
- vis_slot: int32 [8, 524288], P('chan', 'vis'), may hold values from 0 to 15
- vis_wplane: int32 [8, 524288], P('chan', 'vis'), may hold values from 0 to 31
- vis_offset: int32 [2, 8, 524288], P(None, 'chan', 'vis'), may hold values from 0 to 24
Outputs:
- model_step: float32 [2, 256, 1024], P(None, 'vis', 'chan')
- residual: float32 [2, 8, 524288], P(None, 'chan', 'vis')
Inputs may be any that keep to these rules, and one draw needn't show every extreme that they name: `tile_list`: the 16 tiles of one block's list are different and have different owners t // 4.
All inputs are finite; a program needn't handle non-finite values.
Results may differ from a plain program's by a relative error of at most 0.0003.
Values sent between devices are 32-bit elements; how exact they have to be, the bound alone decides.
No kernel may reach another device: no remote copies, remote signals or barrier semaphores. Data moves between devices by JAX's collectives and lax.ppermute only.
A program may use at most 64 MiB of HBM per device.

v0:
```python
import math
import jax
import jax.numpy as jnp
from jax import lax
from jax.sharding import PartitionSpec as P

TILE_SIDE = 32
HIGH = lax.Precision.HIGHEST


def dft_tables(side):
    index = jnp.arange(side, dtype=jnp.int32)
    angle = 2.0 * math.pi / side * (index[:, None] * index[None, :] % side).astype(jnp.float32)
    scale = 1.0 / math.sqrt(side)
    return (jnp.cos(angle) * scale, -jnp.sin(angle) * scale)


def forward(images, cosine, sine):

    def triple(left, right):
        return jnp.einsum("pa,tab,bq->tqp", left, images, right, precision=HIGH)

    return (
        triple(cosine, cosine) - triple(sine, sine),
        triple(cosine, sine) + triple(sine, cosine),
    )


def adjoint(part_re, part_im, cosine, sine):

    def triple(left, middle, right):
        return jnp.einsum("ap,tqp,qb->tab", left, middle, right, precision=HIGH)

    return (
        triple(cosine, part_re, cosine)
        - triple(sine, part_re, sine)
        + triple(sine, part_im, cosine)
        + triple(cosine, part_im, sine)
    )


def place(offset, taps, side):
    rows = jnp.arange(side, dtype=jnp.int32)[:, None]
    shift = rows - offset[None, :]
    total = jnp.zeros((side, offset.shape[0]), jnp.float32)
    for tap in range(taps.shape[0]):
        total = total + jnp.where(shift == tap, taps[tap][None, :], jnp.float32(0.0))
    return total


def crossed(left, right):
    return lax.dot_general(left, right, (((1,), (1,)), ((), ())), precision=HIGH)


def visibility_pass(
    grid_re, grid_im, slot, wplane, off_u, off_v, data_re, data_im, weight, kernels
):
    slots, side = (grid_re.shape[0], grid_re.shape[1])
    planes = kernels.shape[1]
    picker = (jnp.arange(planes, dtype=jnp.int32)[:, None] == wplane[None, :]).astype(jnp.float32)
    taps_re = jnp.dot(kernels[0].T, picker, precision=HIGH)
    taps_im = jnp.dot(kernels[1].T, picker, precision=HIGH)
    a_re = place(off_u, taps_re, side)
    a_im = place(off_u, taps_im, side)
    b_re = place(off_v, taps_re, side)
    b_im = place(off_v, taps_im, side)
    flat_re = grid_re.reshape(slots * side, side)
    flat_im = grid_im.reshape(slots * side, side)
    y_re = jnp.dot(flat_re, a_re, precision=HIGH) - jnp.dot(flat_im, a_im, precision=HIGH)
    y_im = jnp.dot(flat_re, a_im, precision=HIGH) + jnp.dot(flat_im, a_re, precision=HIGH)
    y_re = y_re.reshape(slots, side, -1)
    y_im = y_im.reshape(slots, side, -1)
    owner = (jnp.arange(slots, dtype=jnp.int32)[:, None] == slot[None, :]).astype(jnp.float32)
    pred_re = jnp.sum(owner * jnp.sum(y_re * b_re[None] - y_im * b_im[None], axis=1), axis=0)
    pred_im = jnp.sum(owner * jnp.sum(y_re * b_im[None] + y_im * b_re[None], axis=1), axis=0)
    res_re = weight * (data_re - pred_re)
    res_im = weight * (data_im - pred_im)
    z_re = (owner[:, None, :] * (res_re * b_re + res_im * b_im)[None]).reshape(slots * side, -1)
    z_im = (owner[:, None, :] * (res_im * b_re - res_re * b_im)[None]).reshape(slots * side, -1)
    part_re = crossed(z_re, a_re) + crossed(z_im, a_im)
    part_im = crossed(z_im, a_re) - crossed(z_re, a_im)
    return (res_re, res_im, part_re.reshape(slots, side, side), part_im.reshape(slots, side, side))


def shards(model, kernels, vis_data, vis_weight, tile_list, vis_slot, vis_wplane, vis_offset):
    side = TILE_SIDE
    cells = side * side
    channels = lax.axis_size("chan")
    chan_here = lax.axis_index("chan")
    offsets_all = (jnp.arange(channels, dtype=jnp.float32) - 0.5 * (channels - 1)) / channels
    frequency = jnp.sum(
        jnp.where(jnp.arange(channels, dtype=jnp.int32) == chan_here, offsets_all, jnp.float32(0.0))
    )
    cosine, sine = dft_tables(side)
    listed = tile_list[0, 0]
    slots = listed.shape[0]
    tile_dev = model.shape[1]
    piece_cells = model.shape[2]
    whole = lax.all_gather(model, "chan", axis=2, tiled=True)

    def matches(length):
        return (listed[:, None] == jnp.arange(length, dtype=jnp.int32)[None, :]).astype(jnp.float32)

    image = (whole[0] + frequency * whole[1]).reshape(tile_dev, side, side)
    own_re, own_im = forward(image, cosine, sine)
    packed = jnp.concatenate(
        [own_re.reshape(tile_dev, cells), own_im.reshape(tile_dev, cells)], axis=1
    )
    piece = lax.all_gather(packed, "vis", axis=0, tiled=True)
    chosen = jnp.dot(matches(piece.shape[0]), piece, precision=HIGH)
    grid_re = chosen[:, :cells].reshape(slots, side, side)
    grid_im = chosen[:, cells:].reshape(slots, side, side)
    count = vis_data.shape[2]
    block = min(512, count)
    blocks = count // block

    def rows_of(values):
        return values.reshape(blocks, block)

    sequence = (
        rows_of(vis_slot[0]),
        rows_of(vis_wplane[0]),
        rows_of(vis_offset[0, 0]),
        rows_of(vis_offset[1, 0]),
        rows_of(vis_data[0, 0]),
        rows_of(vis_data[1, 0]),
        rows_of(vis_weight[0]),
    )

    def one_block(carry, inputs):
        slot, wplane, off_u, off_v, data_re, data_im, weight = inputs
        res_re, res_im, part_re, part_im = visibility_pass(
            grid_re, grid_im, slot, wplane, off_u, off_v, data_re, data_im, weight, kernels
        )
        return ((carry[0] + part_re, carry[1] + part_im), (res_re, res_im))

    empty = jnp.zeros((slots, side, side), jnp.float32)
    (acc_re, acc_im), (out_re, out_im) = lax.scan(one_block, (empty, empty), sequence)
    residual = jnp.stack([out_re.reshape(count), out_im.reshape(count)])[:, None, :]
    partial_tiles = jnp.concatenate(
        [acc_re.reshape(slots, cells), acc_im.reshape(slots, cells)], axis=1
    )
    owned = lax.psum_scatter(
        jnp.dot(matches(lax.axis_size("vis") * tile_dev).T, partial_tiles, precision=HIGH),
        "vis",
        scatter_dimension=0,
        tiled=True,
    )
    dirty = adjoint(
        owned[:, :cells].reshape(tile_dev, side, side),
        owned[:, cells:].reshape(tile_dev, side, side),
        cosine,
        sine,
    ).reshape(tile_dev, cells)
    every = lax.all_gather(dirty[None], "chan", axis=0, tiled=True)
    mine = lax.dynamic_slice_in_dim(every, chan_here * piece_cells, piece_cells, 2)
    gradient = jnp.stack(
        [jnp.sum(mine, axis=0), jnp.sum(offsets_all[:, None, None] * mine, axis=0)]
    )
    curvature = jnp.stack([jnp.float32(channels), jnp.sum(offsets_all * offsets_all)])
    model_step = gradient / curvature[:, None, None]
    return (model_step, residual)


def solution(mesh):
    placed = (
        P(None, "vis", "chan"),
        P(),
        P(None, "chan", "vis"),
        P("chan", "vis"),
        P("chan", "vis", None),
        P("chan", "vis"),
        P("chan", "vis"),
        P(None, "chan", "vis"),
    )
    return jax.shard_map(
        shards,
        mesh=mesh,
        in_specs=placed,
        out_specs=(P(None, "vis", "chan"), P(None, "chan", "vis")),
        check_vma=False,
    )
```

profile of v0, /device:TPU:1, one launch (start us, length us, event | category | flops | bytes accessed | tf_op | source)
XLA Modules:
  0.0 474.5 jit_solution(9715506819741355807)
XLA Ops:
  7.9 18.1 %all_gather.9 = f32[2,4,1024]{2,1,0:T(4,128)S(1)} all-gather(f32[2,4,128]{2,1,0:T(4,128)} %param.10), channel_id=1, replica_groups=mesh['vis'=64,'chan'=8] {'chan'}, dimensions={2}, use_global_device_ids=true | all-gather | bytes 36864 | tf_op jit(solution)/shard_map/all_gather | solution.py:99
  34.6 73.3 %all-gather.3.cloned.1.call-done = f32[64,4,2048]{2,1,0:T(4,128)} async-done(((f32[1,4,2048]{2,1,0:T(4,128)}), f32[64,4,2048]{2,1,0:T(4,128)}) %all-gather.3.cloned.1.call-update) | async-done | bytes 2097168 | tf_op jit(solution)/shard_map/all_gather | solution.py:109
  107.9 2.0 reshape.1041
  110.7 171.5 %while.17 = (s32[]{:T(128)}, f32[16,32,32]{1,0,2:T(8,128)S(1)}, f32[16,32,32]{1,0,2:T(8,128)S(1)}, f32[16,512]{1,0:T(8,128)S(1)}, f32[16,512]{1,0:T(8,128)S(1)},...) while((s32[]{:T(128)}, f32[16,32,32]{1,0,2:T(8,128)S(1)}, ...), condition=%wide.region_6.7_spmd.clone, body=%wide.region_1.6_spmd.clone.sunk | while | flops 816292864 | bytes 15255747 | solution.py:138
  114.6 1.4 subtract_reduce_fusion.2
  116.5 1.1 fusion.270
  117.6 1.1 convolution_add_fusion.6
  119.9 1.1 convolution_subtract_fusion.7
  125.3 1.4 subtract_reduce_fusion.2
  127.2 1.1 fusion.270
  128.3 1.1 convolution_add_fusion.6
  130.6 1.1 convolution_subtract_fusion.7
  136.0 1.4 subtract_reduce_fusion.2
  137.9 1.1 fusion.270
  139.0 1.1 convolution_add_fusion.6
  141.4 1.1 convolution_subtract_fusion.7
  146.8 1.4 subtract_reduce_fusion.2
  148.6 1.1 fusion.270
  149.7 1.1 convolution_add_fusion.6
  152.1 1.1 convolution_subtract_fusion.7
  157.5 1.4 subtract_reduce_fusion.2
  159.4 1.1 fusion.270
  160.5 1.1 convolution_add_fusion.6
  162.8 1.1 convolution_subtract_fusion.7
  168.2 1.4 subtract_reduce_fusion.2
  170.1 1.1 fusion.270
  171.2 1.1 convolution_add_fusion.6
  173.5 1.1 convolution_subtract_fusion.7
  178.9 1.4 subtract_reduce_fusion.2
  180.8 1.1 fusion.270
  181.9 1.1 convolution_add_fusion.6
  184.2 1.1 convolution_subtract_fusion.7
  189.6 1.4 subtract_reduce_fusion.2
  191.5 1.1 fusion.270
  192.6 1.1 convolution_add_fusion.6
  195.0 1.1 convolution_subtract_fusion.7
  200.4 1.4 subtract_reduce_fusion.2
  203.3 1.1 convolution_add_fusion.6
  205.7 1.1 convolution_subtract_fusion.7
  211.1 1.4 subtract_reduce_fusion.2
  214.1 1.1 convolution_add_fusion.6
  216.4 1.1 convolution_subtract_fusion.7
  221.8 1.4 subtract_reduce_fusion.2
  224.8 1.1 convolution_add_fusion.6
  227.1 1.1 convolution_subtract_fusion.7
  232.5 1.4 subtract_reduce_fusion.2
  235.5 1.1 convolution_add_fusion.6
  237.8 1.1 convolution_subtract_fusion.7
  243.2 1.4 subtract_reduce_fusion.2
  246.2 1.1 convolution_add_fusion.6
  248.6 1.1 convolution_subtract_fusion.7
  254.0 1.4 subtract_reduce_fusion.2
  256.9 1.1 convolution_add_fusion.6
  259.3 1.1 convolution_subtract_fusion.7
  264.7 1.4 subtract_reduce_fusion.2
  267.7 1.1 convolution_add_fusion.6
  270.0 1.1 convolution_subtract_fusion.7
  275.4 1.4 subtract_reduce_fusion.2
  278.4 1.1 convolution_add_fusion.6
  280.7 1.1 convolution_subtract_fusion.7
  282.9 2.4 fusion.101
  285.3 1.3 dynamic-slice
  289.6 156.2 %all-reduce.3.cloned.1.call-done = f32[256,2048]{1,0:T(8,128)} async-done(((f32[256,2048]{1,0:T(8,128)}), f32[256,2048]{1,0:T(8,128)}) %all-reduce.3.cloned.1.call-update) | async-done | bytes 2097168
  449.8 17.2 %all_gather.11 = f32[8,4,1024]{2,1,0:T(4,128)S(1)} all-gather(f32[1,4,1024]{2,1,0:T(4,128)S(1)} %broadcast_in_dim_reshape.3), channel_id=1, replica_groups=mesh['vis'=64,'chan'=8] {'chan'}, dimensions={0}, use_global_device_ids=true | all-gather | bytes 147456 | tf_op jit(solution)/shard_map/all_gather | solution.py:155
  (481 shorter events, 118.8 us)
Async XLA Ops:
  7.2 24.8 %copy-start.1 = (s32[1,8192]{1,0:T(1,128)S(1)}, s32[1,8192]{1,0:T(1,128)}, u32[]{:S(2)}) copy-start(s32[1,8192]{1,0:T(1,128)} %param.15) | copy-start | bytes 98308
  7.2 25.5 %copy-start.2 = (s32[1,8192]{1,0:T(1,128)S(1)}, s32[1,8192]{1,0:T(1,128)}, u32[]{:S(2)}) copy-start(s32[1,8192]{1,0:T(1,128)} %param.16) | copy-start | bytes 98308
  7.2 26.7 %copy-start.3 = (f32[1,8192]{1,0:T(1,128)S(1)}, f32[1,8192]{1,0:T(1,128)}, u32[]{:S(2)}) copy-start(f32[1,8192]{1,0:T(1,128)} %param.13) | copy-start | bytes 98308
  7.2 100.7 %all-gather.3.cloned.1.call-start = ((), (), s32[]{:S(2)}) async-start(), calls=%async_computation | async-start | bytes 2129920 | tf_op jit(solution)/shard_map/all_gather | solution.py:109
  29.4 416.4 %all-reduce.3.cloned.1.call-start = ((), (), s32[]{:S(2)}) async-start(), calls=%async_computation.1 | async-start | bytes 4194304
  34.6 75.3 %copy-start.4 = (s32[1,1,16]{2,1,0:T(1,128)S(1)}, s32[1,1,16]{2,1,0:T(1,128)}, u32[]{:S(2)}) copy-start(s32[1,1,16]{2,1,0:T(1,128)} %param.14) | copy-start | bytes 196
  109.9 0.9 copy-start
Sparse Core Ops, SparseCore 0:
  29.5 78.3 all-gather.2
  285.4 160.3 all-reduce.2
where the time goes:
time: 475 us
  waiting for transfers between devices  230 us (48%)
  matrix products  155 us (33%)
  blocking collectives  35.3 us (7%)
  local copies, waits for them, and re-layouts  19.6 us (4%)
  other arithmetic  16.9 us (4%)
  between operations  15 us (3%)
    unnamed x3, waiting for transfers between devices  156 us
    all_gather x1, waiting for transfers between devices, shards(): piece = lax.all_gather(packed, 'vis', axis=0, tiled=True)  73.3 us
    dot_general x64, matrix products, crossed(): lax.dot_general(left, right, (((1,), (1,)), ((), ())), precision=HIGH)  70.7 us
    dot_general x16, matrix products, visibility_pass(): jnp.dot(flat_im, a_re, precision=HIGH)  22.7 us
    all_gather x1, blocking collectives, shards(): whole = lax.all_gather(model, 'chan', axis=2, tiled=True)  18.1 us
    all_gather x1, blocking collectives, shards(): every = lax.all_gather(dirty[None], 'chan', axis=0, tiled=True)  17.2 us
    dot_general x16, matrix products, visibility_pass(): jnp.dot(flat_im, a_im, precision=HIGH)  16.9 us
    dot_general x16, matrix products, visibility_pass(): jnp.dot(flat_re, a_re, precision=HIGH)  16.4 us
  transfers between devices with their start and end apart: 2, of which 2 were waited for; matrix products, arithmetic and copies ran while one was open for 2% of the time, Pallas kernels for 0%

commit v1 on v0

--- a/solution.py
+++ b/solution.py
@@ -96,7 +96,12 @@
     slots = listed.shape[0]
     tile_dev = model.shape[1]
     piece_cells = model.shape[2]
-    whole = lax.all_gather(model, "chan", axis=2, tiled=True)
+    ring = [model]
+    for hop in range(7):
+        ring.append(lax.ppermute(ring[-1], "chan", [(dev, (dev + 1) % 8) for dev in range(8)]))
+    whole = jnp.roll(
+        jnp.concatenate(ring[::-1], axis=2), (lax.axis_index("chan") + 1) * ring[0].shape[2], axis=2
+    )
 
     def matches(length):
         return (listed[:, None] == jnp.arange(length, dtype=jnp.int32)[None, :]).astype(jnp.float32)

time: 475 us -> 492 us (1.036)
  waiting for transfers between devices: 230 us -> 261 us
  blocking collectives: 35.3 us -> 17.2 us
    ppermute x0 -> x7, waiting for transfers between devices: none -> 30 us  [shards(): lax.ppermute(ring[-1], 'chan', [(dev, (dev + 1) % 8) for dev in range(8)])]
    all_gather x1 -> x0, blocking collectives: 18.1 us -> none  [shards(): whole = lax.all_gather(model, 'chan', axis=2, tiled=True)]
  transfers between devices with their start and end apart: 2 -> 9, of which waited for: 2 -> 9; matrix products, arithmetic and copies ran while one was open for 2% -> 2% of each run, Pallas kernels for 0% -> 0%
where the time goes in v1:
time: 492 us
  waiting for transfers between devices  261 us (53%)
  matrix products  155 us (32%)
  local copies, waits for them, and re-layouts  21.1 us (4%)
  blocking collectives  17.2 us (3%)
  other arithmetic  16.9 us (3%)
  between operations  15 us (3%)
    unnamed x3, waiting for transfers between devices  156 us
    all_gather x1, waiting for transfers between devices, shards(): piece = lax.all_gather(packed, 'vis', axis=0, tiled=True)  74.5 us
    dot_general x64, matrix products, crossed(): lax.dot_general(left, right, (((1,), (1,)), ((), ())), precision=HIGH)  70.7 us
    ppermute x7, waiting for transfers between devices, shards(): lax.ppermute(ring[-1], 'chan', [(dev, (dev + 1) % 8) for dev in range(8)])  30 us
    dot_general x16, matrix products, visibility_pass(): jnp.dot(flat_im, a_re, precision=HIGH)  22.7 us
    all_gather x1, blocking collectives, shards(): every = lax.all_gather(dirty[None], 'chan', axis=0, tiled=True)  17.2 us
    dot_general x16, matrix products, visibility_pass(): jnp.dot(flat_im, a_im, precision=HIGH)  16.9 us
    dot_general x16, matrix products, visibility_pass(): jnp.dot(flat_re, a_re, precision=HIGH)  16.4 us
  transfers between devices with their start and end apart: 9, of which 9 were waited for; matrix products, arithmetic and copies ran while one was open for 2% of the time, Pallas kernels for 0%

profile of v1, /device:TPU:1, one launch (start us, length us, event | category | flops | bytes accessed | tf_op | source)
XLA Modules:
  0.0 491.8 jit_solution(10047747993569219748)
XLA Ops:
  7.2 2.6 collective-permute-start
  9.9 5.2 %collective-permute-done = f32[2,4,128]{2,1,0:T(4,128)S(1)} collective-permute-done((f32[2,4,128]{2,1,0:T(4,128)}, f32[2,4,128]{2,1,0:T(4,128)S(1)}, u32[]{:S(2)}, u32[]{:S(2)}) %collective-permute-start) | collective-permute-done | bytes 4128 | tf_op jit(solution)/shard_map/ppermute | solution.py:101
  15.0 4.2 collective-permute-done.1
  19.2 4.2 collective-permute-done.2
  23.5 4.2 collective-permute-done.3
  27.7 4.2 collective-permute-done.4
  32.0 4.2 collective-permute-done.5
  36.8 3.6 collective-permute-done.6
  50.6 74.5 %all-gather.3.cloned.1.call-done = f32[64,4,2048]{2,1,0:T(4,128)} async-done(((f32[1,4,2048]{2,1,0:T(4,128)}), f32[64,4,2048]{2,1,0:T(4,128)}) %all-gather.3.cloned.1.call-update) | async-done | bytes 2097168 | tf_op jit(solution)/shard_map/all_gather | solution.py:114
  125.1 2.0 reshape.1041
  128.0 171.5 %while.17 = (s32[]{:T(128)}, f32[16,32,32]{1,0,2:T(8,128)S(1)}, f32[16,32,32]{1,0,2:T(8,128)S(1)}, f32[16,512]{1,0:T(8,128)S(1)}, f32[16,512]{1,0:T(8,128)S(1)},...) while((s32[]{:T(128)}, f32[16,32,32]{1,0,2:T(8,128)S(1)}, ...), condition=%wide.region_6.7_spmd.clone, body=%wide.region_1.6_spmd.clone.sunk | while | flops 816292864 | bytes 15255747 | solution.py:143
  131.8 1.4 subtract_reduce_fusion.2
  134.8 1.1 convolution_add_fusion.6
  137.1 1.1 convolution_subtract_fusion.7
  142.5 1.4 subtract_reduce_fusion.2
  144.4 1.1 fusion.270
  145.5 1.1 convolution_add_fusion.6
  147.9 1.1 convolution_subtract_fusion.7
  153.3 1.4 subtract_reduce_fusion.2
  156.2 1.1 convolution_add_fusion.6
  158.6 1.1 convolution_subtract_fusion.7
  164.0 1.4 subtract_reduce_fusion.2
  167.0 1.1 convolution_add_fusion.6
  169.3 1.1 convolution_subtract_fusion.7
  174.7 1.4 subtract_reduce_fusion.2
  177.7 1.1 convolution_add_fusion.6
  180.0 1.1 convolution_subtract_fusion.7
  185.4 1.4 subtract_reduce_fusion.2
  188.4 1.1 convolution_add_fusion.6
  190.7 1.1 convolution_subtract_fusion.7
  196.1 1.4 subtract_reduce_fusion.2
  199.1 1.1 convolution_add_fusion.6
  201.5 1.1 convolution_subtract_fusion.7
  206.9 1.4 subtract_reduce_fusion.2
  209.8 1.1 convolution_add_fusion.6
  212.2 1.1 convolution_subtract_fusion.7
  217.6 1.4 subtract_reduce_fusion.2
  220.6 1.1 convolution_add_fusion.6
  222.9 1.1 convolution_subtract_fusion.7
  228.3 1.4 subtract_reduce_fusion.2
  231.3 1.1 convolution_add_fusion.6
  233.6 1.1 convolution_subtract_fusion.7
  239.0 1.4 subtract_reduce_fusion.2
  242.0 1.1 convolution_add_fusion.6
  244.3 1.1 convolution_subtract_fusion.7
  249.7 1.4 subtract_reduce_fusion.2
  252.7 1.1 convolution_add_fusion.6
  255.1 1.1 convolution_subtract_fusion.7
  260.5 1.4 subtract_reduce_fusion.2
  263.4 1.1 convolution_add_fusion.6
  265.8 1.1 convolution_subtract_fusion.7
  271.2 1.4 subtract_reduce_fusion.2
  274.2 1.1 convolution_add_fusion.6
  276.5 1.1 convolution_subtract_fusion.7
  281.9 1.4 subtract_reduce_fusion.2
  284.9 1.1 convolution_add_fusion.6
  287.2 1.1 convolution_subtract_fusion.7
  292.6 1.4 subtract_reduce_fusion.2
  295.6 1.1 convolution_add_fusion.6
  297.9 1.1 convolution_subtract_fusion.7
  300.1 2.4 fusion.101
  302.5 1.3 dynamic-slice
  306.8 156.3 %all-reduce.3.cloned.1.call-done = f32[256,2048]{1,0:T(8,128)} async-done(((f32[256,2048]{1,0:T(8,128)}), f32[256,2048]{1,0:T(8,128)}) %all-reduce.3.cloned.1.call-update) | async-done | bytes 2097168
  467.1 17.2 %all_gather.7 = f32[8,4,1024]{2,1,0:T(4,128)S(1)} all-gather(f32[1,4,1024]{2,1,0:T(4,128)S(1)} %broadcast_in_dim_reshape.3), channel_id=1, replica_groups=mesh['vis'=64,'chan'=8] {'chan'}, dimensions={0}, use_global_device_ids=true | all-gather | bytes 147456 | tf_op jit(solution)/shard_map/all_gather | solution.py:160
  (510 shorter events, 127.9 us)
Async XLA Ops:
  7.2 40.8 %copy-start.1 = (s32[1,8192]{1,0:T(1,128)S(1)}, s32[1,8192]{1,0:T(1,128)}, u32[]{:S(2)}) copy-start(s32[1,8192]{1,0:T(1,128)} %param.15) | copy-start | bytes 98308
  7.2 41.5 %copy-start.2 = (s32[1,8192]{1,0:T(1,128)S(1)}, s32[1,8192]{1,0:T(1,128)}, u32[]{:S(2)}) copy-start(s32[1,8192]{1,0:T(1,128)} %param.16) | copy-start | bytes 98308
  7.2 42.7 %copy-start.3 = (f32[1,8192]{1,0:T(1,128)S(1)}, f32[1,8192]{1,0:T(1,128)}, u32[]{:S(2)}) copy-start(f32[1,8192]{1,0:T(1,128)} %param.13) | copy-start | bytes 98308
  7.2 117.9 %all-gather.3.cloned.1.call-start = ((), (), s32[]{:S(2)}) async-start(), calls=%async_computation | async-start | bytes 2129920 | tf_op jit(solution)/shard_map/all_gather | solution.py:114
  7.2 7.8 %collective-permute-start = (f32[2,4,128]{2,1,0:T(4,128)}, f32[2,4,128]{2,1,0:T(4,128)S(1)}, u32[]{:S(2)}, u32[]{:S(2)}) collective-permute-start(f32[2,4,128]{2,1,0:T(4,128)} %param.10), channel_id=1, source_target_pairs={{0,1},{1,2},{2,3},{3,4},{4,5},{5,6},{6,7},{7,0},{8,9},{9,10},{10,1... | collective-permute-start | bytes 12296 | tf_op jit(solution)/shard_map/ppermute | solution.py:101
  15.0 4.2 collective-permute-start.1
  19.2 4.2 collective-permute-start.2
  23.5 4.2 collective-permute-start.3
  27.7 4.2 collective-permute-start.4
  32.0 4.2 collective-permute-start.5
  36.2 4.2 collective-permute-start.6
  45.4 417.7 %all-reduce.3.cloned.1.call-start = ((), (), s32[]{:S(2)}) async-start(), calls=%async_computation.1 | async-start | bytes 4194304
  50.6 76.5 %copy-start.4 = (s32[1,1,16]{2,1,0:T(1,128)S(1)}, s32[1,1,16]{2,1,0:T(1,128)}, u32[]{:S(2)}) copy-start(s32[1,1,16]{2,1,0:T(1,128)} %param.14) | copy-start | bytes 196
  127.1 0.9 copy-start
Sparse Core Ops, SparseCore 0:
  45.6 79.5 all-gather.2
  302.6 160.4 all-reduce.2
